TPU v7x, 32 devices: a whole 2x2x4 slice. The times are simulated.
32 devices in a mesh: dp: 8 (over z, y), tensor: 4 (over x, core).
Axes of the slice: x: 2, y: 2, z: 4, core: 2. Of those that a mesh axis runs over, the one named last changes fastest.
Arguments:
- hidden: bfloat16 [1536, 4096], P('dp'), may hold values from -64 to 64
- output_weight: bfloat16 [4096, 128256], P(None, ('dp', 'tensor')), may hold values from -0.109375 to 0.109375
- targets: int32 [1536], P('dp'), may hold values from 0 to 128255
- labels: int32 [1536, 1], P('dp'), may hold values from 0 to 63; in each aligned block of 192 rows (0 to 191, 192 to 383, ...) at most 12 rows name the same one
- prev_scores: float32 [64], P('dp'), may hold values from -12 to 320
- prev_probs: float32 [64], P('dp')
- next_domains: int32 [128], P('dp'), may hold values from 0 to 63
Outputs:
- token_loss: float32 [1536], P(('dp', 'tensor'))
- new_scores: float32 [64], P('dp')
- log_probs: float32 [64], replicated
- sample_weights: float32 [128], P('dp')
Inputs may be any that keep to these rules, and one draw needn't show every extreme that they name: `labels`: within the 192 tokens of one index of dp no domain appears more than 12 times; every domain appears somewhere in the batch.
All inputs are finite; a program needn't handle non-finite values.
Results may differ from a plain program's by a relative error of at most 0.0003.
Values may be sent and summed in bfloat16 or wider, within the bound.
No kernel may reach another device: no remote copies, remote signals or barrier semaphores. Data moves between devices by JAX's collectives and lax.ppermute only.
A program may use at most 128 MiB of HBM per device.

v0:
```python
import functools
import math

import jax
import jax.numpy as jnp
from jax import lax
from jax.experimental import pallas as pl
from jax.experimental.pallas import tpu as pltpu
from jax.sharding import PartitionSpec as P

K = 64
STEP = 2000
LOW = -3.0e38
TILE = 512
GROUP = 2
FEW = 256
NT = (((1,), (1,)), ((), ()))
AXES = ("dp", "tensor")


def exploration_rates():
    earlier = min(1.0 / K, math.sqrt(math.log(K) / (K * (STEP - 1))))
    current = min(1.0 / K, math.sqrt(math.log(K) / (K * STEP)))
    return (earlier, current)


def at_ring(place, count):
    place = lax.rem(place + count, count)
    return jnp.where(place < count // 2, 2 * place, 2 * (count - 1 - place) + 1)


def ring_place(index, count):
    half = lax.div(index, 2)
    return jnp.where(lax.rem(index, 2) == 0, half, count - 1 - half)


def each_tile(groups, limit, visit):
    number = 0
    for place, group in enumerate(groups):
        count = group.shape[0] // TILE
        turn = limit if count % limit == 0 else count

        def body(i, carry, group=group, number=number, turn=turn, final=place == len(groups) - 1):
            for j in range(turn):
                tile = i * turn + j
                visit(group.at[pl.ds(pl.multiple_of(tile * TILE, TILE), TILE), :], number + tile, final)
            return carry

        lax.fori_loop(0, count // turn, body, 0)
        number += count


def slice_stats(rows, walk, vocab, wanted, vocab_offset, top, total, picked):
    count = rows.shape[0]
    top[...] = jnp.full_like(top, LOW)
    total[...] = jnp.zeros_like(total)
    picked[...] = jnp.zeros_like(picked)
    lane = lax.broadcasted_iota(jnp.int32, (count, 128), 1)
    wanted = jnp.broadcast_to(wanted, (count, 128)) - vocab_offset - lane

    def visit(weights, tile, final):
        logits = lax.dot_general(rows, weights[...], NT, preferred_element_type=jnp.float32)
        start = tile * TILE
        parts = []
        chosen = picked[...]
        for i in range(0, TILE, 128):
            part = logits[:, i : i + 128]
            found = wanted == start + i
            if final:
                inside = lane < vocab - start - i
                part = jnp.where(inside, part, LOW)
                found = found & inside
            chosen = chosen + jnp.where(found, part, 0.0)
            parts.append(part)
        picked[...] = chosen
        before = top[...]
        now = before
        for part in parts:
            now = jnp.maximum(now, part)
        added = total[...] * jnp.exp(before - now)
        for part in parts:
            added = added + jnp.exp(part - now)
        top[...] = now
        total[...] = added

    walk(visit)
    largest = jnp.max(top[...], axis=1, keepdims=True)
    summed = jnp.sum(total[...] * jnp.exp(top[...] - largest), axis=1, keepdims=True)
    pick = jnp.sum(picked[...], axis=1, keepdims=True)
    both = jnp.where(lane == 0, largest + jnp.log(summed), pick)
    if count % 128:
        both = jnp.concatenate([both, jnp.zeros((-count % 128, 128), jnp.float32)], axis=0)
    return jnp.transpose(both)[:8]


def few_stats(rows, walk, vocab, wanted, vocab_offset, top, total, picked):
    count = rows.shape[0]
    top[...] = jnp.full_like(top, LOW)
    total[...] = jnp.zeros_like(total)
    picked[...] = jnp.zeros_like(picked)

    def visit(weights, tile, final):
        logits = lax.dot_general(weights[...], rows, NT, preferred_element_type=jnp.float32)
        start = tile * TILE
        number = lax.broadcasted_iota(jnp.int32, logits.shape, 0)
        if final:
            logits = jnp.where(number < vocab - start, logits, LOW)
        found = number == wanted - vocab_offset - start
        if final:
            found = found & (number < vocab - start)
        found = jnp.where(found, logits, 0.0)
        logits = logits.reshape(TILE // 8, 8, count)
        picked[...] += jnp.sum(found.reshape(TILE // 8, 8, count), axis=0)
        before = top[...]
        now = jnp.maximum(before, jnp.max(logits, axis=0))
        total[...] = total[...] * jnp.exp(before - now) + jnp.sum(jnp.exp(logits - now[None]), axis=0)
        top[...] = now

    walk(visit)
    largest = jnp.max(top[...], axis=0, keepdims=True)
    summed = jnp.sum(total[...] * jnp.exp(top[...] - largest), axis=0, keepdims=True)
    return largest + jnp.log(summed), jnp.sum(picked[...], axis=0, keepdims=True)


def column_from(row):
    size = row.shape[1]
    same = lax.broadcasted_iota(jnp.int32, (size, size), 0) == lax.broadcasted_iota(jnp.int32, (size, size), 1)
    return jnp.sum(jnp.where(same, row, 0), axis=1, keepdims=True)


def offset_of(place, tensor_count, vocab):
    return (place[0] * tensor_count + place[1]) * vocab


def first_kernel(tensor_count, place, rows, target, ending, weight, out, *rest):
    vocab, width = weight.shape
    groups, arrived, scratch = rest[:-4], rest[-4], rest[-3:]
    tiles = [group.at[pl.ds(i, TILE), :] for group in groups for i in range(0, group.shape[0], TILE)]
    last = len(tiles) - 1
    copies = [
        pltpu.make_async_copy(weight.at[pl.ds(i * TILE, TILE), :], tiles[i], arrived.at[i]) for i in range(last)
    ]
    for copy in copies:
        copy.start()
    tiles[last][...] = ending[...]

    def walk(visit):
        def arriving(weights, tile, final):
            @pl.when(tile < last)
            def _():
                pltpu.make_async_copy(tiles[0], tiles[0], arrived.at[tile]).wait()

            visit(weights, tile, final)

        each_tile(groups, 1, arriving)

    wanted = column_from(target[...])
    out[...] = slice_stats(rows[...], walk, vocab, wanted, offset_of(place, tensor_count, vocab), *scratch)


def pair_kernel(tensor_count, vocab, turn, place, one, two, target_one, target_two, *rest):
    groups, out, scratch = rest[:-4], rest[-4], rest[-3:]
    rows = jnp.concatenate([one[...], two[...]], axis=0)
    offset = offset_of(place, tensor_count, vocab)
    walk = functools.partial(each_tile, groups, turn)
    if rows.shape[0] > FEW:
        wanted = jnp.concatenate([column_from(target_one[...]), column_from(target_two[...])], axis=0)
        out[...] = slice_stats(rows, walk, vocab, wanted, offset, *scratch)
    else:
        wanted = jnp.concatenate([target_one[...], target_two[...]], axis=1)
        logs, picks = few_stats(rows, walk, vocab, wanted, offset, *scratch)
        out[0:1, : rows.shape[0]] = logs
        out[1:2, : rows.shape[0]] = picks


def half_kernel(place, block, target, out, target_out):
    size = out.shape[0]
    core = lax.rem(place[1], 2)
    out[...] = block[pl.ds(pl.multiple_of(core * size, size), size), :]
    target_out[...] = jnp.where(core == 0, target[:, :size], target[:, size:])


def table_kernel(size, place, own, *refs):
    stats, outs = refs[:-2], refs[-2:]
    half, piece = size // 2, size // 4
    core = lax.rem(place[1], 2)
    for theirs, out in enumerate(outs):
        out[...] = jnp.zeros_like(out)
        for kind in range(2):
            for step, table in enumerate(stats):
                row = 2 * step + kind
                out[row : row + 1, :size] = table[kind : kind + 1, theirs * size : (theirs + 1) * size]
            part = jnp.where(core == theirs, own[kind : kind + 1, :half], own[kind : kind + 1, half:size])
            for i in range(2):
                row = 2 * kind + i
                out[row : row + 1, size : size + piece] = part[:, i * piece : (i + 1) * piece]


def pack_kernel(size, steps, place, labels, scores, probs, mine, got, last, out, table):
    core = lax.rem(place[1], 2)
    row = lax.broadcasted_iota(jnp.int32, mine.shape, 0)
    lane = lax.broadcasted_iota(jnp.int32, mine.shape, 1)
    logs = jnp.where(lane < size, lax.rem(row, 2), row // 2) == 0
    one, two = mine[...], got[...]
    most = jnp.maximum(one, two)
    both = most + jnp.log(jnp.exp(one - most) + jnp.exp(two - most))
    table[...] = jnp.where(logs, both, one + two)
    for kind in range(2):
        rows = last[kind : kind + 1, :size]
        swapped = jnp.concatenate([rows[:, size // 2 :], rows[:, : size // 2]], axis=1)
        table[2 * steps + kind : 2 * steps + kind + 1, :size] = jnp.where(core == 0, rows, swapped)
    rest = table.shape[1] - size
    pieces = size // rest
    for i in range(pieces):
        table[4 + i : 5 + i, size:] = labels[:, i * rest : (i + 1) * rest].astype(jnp.float32)
    owned = scores.shape[1]
    table[4 + pieces : 5 + pieces, size : size + owned] = scores[...]
    table[4 + pieces : 5 + pieces, size + owned : size + 2 * owned] = probs[...]
    out[...] = jnp.broadcast_to(table[...][None], out.shape)


def row_of(column):
    size = column.shape[0]
    same = lax.broadcasted_iota(jnp.int32, (size, size), 0) == lax.broadcasted_iota(jnp.int32, (size, size), 1)
    return jnp.sum(jnp.where(same, column, 0.0), axis=0, keepdims=True)


def last_kernel(order, tensor_count, place, stats, domains, loss_out, score_out, log_out, weight_out, kept, kept_scores):
    dp_index, tensor_index = place[0], place[1]
    groups, size = kept.shape
    share = loss_out.shape[1]
    owned = score_out.shape[1]
    rest = stats.shape[2] - size
    pieces = size // rest
    piece = size // 4
    steps = groups // 2 - 1
    ring = {index: p for p, index in enumerate(order)}

    def rows_of(away, tensor, row):
        sources = [order[(ring[i] + away) % groups] * tensor_count + tensor for i in range(groups)]
        return jnp.concatenate([stats[d, row : row + 1, :size] for d in sources], axis=0)

    def own_rows(tensor, row):
        parts = []
        for i in range(groups):
            d = i * tensor_count + tensor
            parts.append(
                jnp.concatenate(
                    [stats[d + c, row + j : row + j + 1, size : size + piece] for c in range(2) for j in range(2)], axis=1
                )
            )
        return jnp.concatenate(parts, axis=0)

    tables = []
    for tensor in range(0, tensor_count, 2):
        tables.append((own_rows(tensor, 0), own_rows(tensor, 2)))
        for c in range(2):
            for step in range(1, steps + 1):
                away = step if c == 0 else -step
                tables.append(tuple(rows_of(away, tensor + c, 2 * step - 2 + kind) for kind in range(2)))
            tables.append(tuple(rows_of(steps + 1, tensor + c, 2 * steps + kind) for kind in range(2)))
    overall = functools.reduce(jnp.maximum, [logs for logs, _ in tables])
    total = sum(jnp.exp(logs - overall) for logs, _ in tables)
    loss = overall + jnp.log(total) - sum(picks for _, picks in tables)
    kept[...] = loss
    own = kept[pl.ds(dp_index, 1), :]
    picked = own[:, :share]
    for i in range(1, tensor_count):
        picked = jnp.where(tensor_index == i, own[:, i * share : (i + 1) * share], picked)
    loss_out[...] = picked
    number = lax.broadcasted_iota(jnp.int32, (K, size), 0).astype(jnp.float32)
    place_of = lax.broadcasted_iota(jnp.int32, (K, owned), 0) - lax.broadcasted_iota(jnp.int32, (K, owned), 1)
    sums = jnp.zeros((K, size), jnp.float32)
    counts = jnp.zeros((K, size), jnp.float32)
    scores = jnp.zeros((K, owned), jnp.float32)
    before = jnp.zeros((K, owned), jnp.float32)
    for i in range(groups):
        source = i * tensor_count
        label = jnp.concatenate([stats[source, 4 + j : 5 + j, size:] for j in range(pieces)], axis=1)
        match = number == label
        sums = sums + jnp.where(match, loss[i : i + 1, :], 0.0)
        counts = counts + jnp.where(match, 1.0, 0.0)
        here = place_of == i * owned
        scores = scores + jnp.where(here, stats[source, 4 + pieces : 5 + pieces, size : size + owned], 0.0)
        before = before + jnp.where(here, stats[source, 4 + pieces : 5 + pieces, size + owned : size + 2 * owned], 0.0)
    sums = jnp.sum(sums, axis=1, keepdims=True)
    counts = jnp.sum(counts, axis=1, keepdims=True)
    scores = jnp.sum(scores, axis=1, keepdims=True)
    before = jnp.sum(before, axis=1, keepdims=True)
    earlier, current = exploration_rates()
    new = current / earlier * scores + current * (sums / counts) / before
    kept_scores[...] = jnp.broadcast_to(new, kept_scores.shape)
    score_out[...] = row_of(kept_scores[pl.ds(pl.multiple_of(dp_index * owned, owned), owned), :][:, :1])
    weights = jnp.exp(new - jnp.max(new, axis=0, keepdims=True))
    probs = (1.0 - K * current) * (weights / jnp.sum(weights, axis=0, keepdims=True)) + current
    log_out[...] = row_of(jnp.log(probs))
    known = lax.broadcasted_iota(jnp.int32, (K, domains.shape[1]), 0) == domains[...]
    weight_out[...] = 1.0 / (K * jnp.sum(jnp.where(known, probs, 0.0), axis=0, keepdims=True))


def body(hidden, output_weight, targets, labels, prev_scores, prev_probs, next_domains):
    size, width = hidden.shape
    vocab = output_weight.shape[1]
    dp_count = lax.axis_size("dp")
    tensor_count = lax.axis_size("tensor")
    devices = dp_count * tensor_count
    owned = prev_scores.shape[0]
    steps = dp_count // 2 - 1
    place = jnp.stack([lax.axis_index("dp"), lax.axis_index("tensor")]).astype(jnp.int32)
    order = [2 * i for i in range(dp_count // 2)] + [2 * i + 1 for i in reversed(range(dp_count // 2))]
    along = []
    for p in range(dp_count):
        for t in range(tensor_count):
            to = order[(p + 1 - 2 * (t % 2)) % dp_count]
            along.append((order[p] * tensor_count + t, to * tensor_count + t))
    across = [(t, t ^ 1) for t in range(tensor_count)]

    smem = pl.BlockSpec(memory_space=pltpu.SMEM)
    vmem = pl.BlockSpec(memory_space=pltpu.VMEM)
    whole = pl.BlockSpec(memory_space=pl.ANY)
    fixed = lambda x: pltpu.with_memory_space_constraint(x, pltpu.VMEM)
    limit = pltpu.CompilerParams(vmem_limit_bytes=12 << 20)

    def up_to(count, unit):
        return -(-count // unit) * unit

    full = (vocab - 1) // TILE
    weight = output_weight.T
    groups = [
        pltpu.VMEM((min(GROUP, full + 1 - i) * TILE, width), weight.dtype) for i in range(0, full + 1, GROUP)
    ]

    def stats_of(blocks, wanted, kept, turn=0):
        rows = sum(block.shape[0] for block in blocks)
        first = not kept
        table = jax.ShapeDtypeStruct((8, up_to(rows, 128)), jnp.float32)
        sums = pltpu.VMEM((rows, 128) if first or rows > FEW else (8, rows), jnp.float32)
        return pl.pallas_call(
            functools.partial(first_kernel, tensor_count) if first else functools.partial(pair_kernel, tensor_count, vocab, turn),
            grid=(1,),
            in_specs=[smem]
            + [vmem] * (2 * len(blocks))
            + ([pl.BlockSpec((TILE, width), lambda i: (full, 0)), whole] if first else [vmem] * len(kept)),
            out_specs=[vmem] * (1 + len(groups)) if first else vmem,
            out_shape=[table] + groups if first else table,
            scratch_shapes=([pltpu.SemaphoreType.DMA((max(full, 1),))] if first else []) + [sums] * 3,
            compiler_params=limit,
            cost_estimate=pl.CostEstimate(
                flops=2 * rows * width * vocab, bytes_accessed=2 * width * vocab, transcendentals=rows * vocab
            ),
        )(place, *[fixed(x) for x in blocks], *wanted, *([weight, weight] if first else [fixed(x) for x in kept]))

    def half(block, wanted):
        return pl.pallas_call(
            half_kernel,
            in_specs=[smem, vmem, vmem],
            out_specs=[vmem] * 2,
            out_shape=[
                pltpu.VMEM((size // 2, width), block.dtype),
                jax.ShapeDtypeStruct((1, size // 2), wanted.dtype),
            ],
            compiler_params=limit,
        )(place, fixed(block), wanted)

    def moved(axes, way, *arrays):
        return [lax.ppermute(x, axes, way) for x in arrays]

    block, wanted = hidden, targets[None, :]
    coming = moved(AXES, along, block, wanted)
    stats, *kept = stats_of([block], [wanted], [])
    gathered = [stats]
    shape = (max(2 * steps + 2, 8), up_to(size, 128))
    for step in range(1, steps + 2):
        block, wanted, gathered[-1] = lax.optimization_barrier((*coming, gathered[-1]))
        other, wanted_other = moved("tensor", across, block, wanted)
        if step <= steps:
            coming = moved(AXES, along, *((block, wanted) if step < steps else half(block, wanted)))
        else:
            mine, theirs = pl.pallas_call(
                functools.partial(table_kernel, size),
                in_specs=[smem] + [vmem] * len(gathered),
                out_specs=[vmem] * 2,
                out_shape=[jax.ShapeDtypeStruct(shape, jnp.float32)] * 2,
                compiler_params=limit,
            )(place, *gathered)
            [got] = moved("tensor", across, theirs)
        gathered.append(stats_of([block, other], [wanted, wanted_other], kept, GROUP if step == steps else 1))

    table = pl.pallas_call(
        functools.partial(pack_kernel, size, steps),
        in_specs=[smem] + [vmem] * 6,
        out_specs=vmem,
        out_shape=jax.ShapeDtypeStruct((devices, *shape), jnp.float32),
        scratch_shapes=[pltpu.VMEM(shape, jnp.float32)],
        compiler_params=limit,
    )(place, labels.reshape(1, size), prev_scores[None, :], prev_probs[None, :], mine, got, gathered[-1])
    every = lax.all_to_all(table, AXES, split_axis=0, concat_axis=0, tiled=True)

    loss, scores, logs, weights = pl.pallas_call(
        functools.partial(last_kernel, order, tensor_count),
        in_specs=[smem, vmem, vmem],
        out_specs=[vmem] * 4,
        out_shape=[
            jax.ShapeDtypeStruct((1, size // tensor_count), jnp.float32),
            jax.ShapeDtypeStruct((1, owned), jnp.float32),
            jax.ShapeDtypeStruct((1, K), jnp.float32),
            jax.ShapeDtypeStruct((1, next_domains.shape[0]), jnp.float32),
        ],
        scratch_shapes=[pltpu.VMEM((dp_count, size), jnp.float32), pltpu.VMEM((K, 128), jnp.float32)],
        compiler_params=pltpu.CompilerParams(vmem_limit_bytes=24 << 20),
    )(place, every, next_domains[None, :])
    return (loss[0], scores[0], logs[0], weights[0])


def solution(mesh):
    placed = (
        P("dp", None),
        P(None, AXES),
        P("dp"),
        P("dp", None),
        P("dp"),
        P("dp"),
        P("dp"),
    )
    return jax.shard_map(
        body,
        mesh=mesh,
        in_specs=placed,
        out_specs=(P(AXES), P("dp"), P(), P("dp")),
        check_vma=False,
    )
```

profile of v0, /device:TPU:0, one launch (start us, length us, event | category | flops | bytes accessed | tf_op | source)
XLA Modules:
  0.0 116.1 jit_solution(15060046673974552645)
XLA Ops:
  0.6 3.1 %collective-permute-start = (bf16[192,4096]{1,0:T(8,128)(2,1)}, bf16[192,4096]{1,0:T(8,128)(2,1)}, u32[]{:S(2)}, u32[]{:S(2)}) collective-permute-start(bf16[192,4096]{1,0:T(8,128)(2,1)} %rows.1), channel_id=1, source_target_pairs={{0,8},{1,5},{2,10},{3,7},{8,16},{9,1},{10,18},{11,3},{16,24},{17,9... | collective-permute-start | bytes 4718600 | tf_op jit(solution)/shard_map/ppermute | solution.py:366
  3.7 1.6 %collective-permute-start.1 = (s32[1,192]{1,0:T(1,128)}, s32[1,192]{1,0:T(1,128)S(1)}, u32[]{:S(2)}, u32[]{:S(2)}) collective-permute-start(s32[1,192]{1,0:T(1,128)} %bitcast.13), channel_id=1, source_target_pairs={{0,8},{1,5},{2,10},{3,7},{8,16},{9,1},{10,18},{11,3},{16,24},{17,9... | collective-permute-start | bytes 2312 | tf_op jit(solution)/shard_map/ppermute | solution.py:366
  5.3 0.1 pad_add_fusion.place
  5.4 1.4 %copy-done = bf16[192,4096]{1,0:T(8,128)(2,1)S(1)} copy-done((bf16[192,4096]{1,0:T(8,128)(2,1)S(1)}, bf16[192,4096]{1,0:T(8,128)(2,1)}, u32[]{:S(2)}) %copy-start) | copy-done | bytes 1572888
  6.8 0.7 copy-done.2
  7.4 17.3 %shard_map.102 = (f32[8,256]{1,0:T(8,128)S(1)}, bf16[1024,4096]{1,0:T(8,128)(2,1)S(1)}, bf16[1024,4096]{1,0:T(8,128)(2,1)S(1)}, bf16[1024,4096]{1,0:T(8,128)(2,1)S(1)}, bf16[1024,4096]{1,0:T(8,128)(2,1)S(1)}) custom-call(s32[2]{0:T(128)S(1)} %pad_add_fusion.place, bf16[192,4096]{1,0:T(8,128)(2,1)S(1)} %copy-done, s32[1,192]{1,0:T(1,128)S(1)} %bitcast.14, ...), custom_call_target="tpu_custom_call" | custom-call | flops 6304038912 | bytes 32833536 | tf_op jit(solution)/shard_map/pallas_call | solution.py:338
  24.7 0.0 collective-permute-done.1.target_one
  24.8 0.0 collective-permute-done.one
  24.8 0.1 collective-permute-start.4
  24.8 1.6 %collective-permute-start.2 = (bf16[192,4096]{1,0:T(8,128)(2,1)}, bf16[192,4096]{1,0:T(8,128)(2,1)S(1)}, u32[]{:S(2)}, u32[]{:S(2)}) collective-permute-start(bf16[192,4096]{1,0:T(8,128)(2,1)} %collective-permute-done.one), channel_id=1, source_target_pairs={{0,8},{1,5},{2,10},{3,7},{8,16},{9,1},{10,18},{11,3},{16,24},{17,9... | collective-permute-start | bytes 4718600 | tf_op jit(solution)/shard_map/ppermute | solution.py:366
  26.5 0.0 collective-permute-start.5
  26.5 1.5 %collective-permute-start.3 = (s32[1,192]{1,0:T(1,128)S(1)}, s32[1,192]{1,0:T(1,128)S(1)}, u32[]{:S(2)}, u32[]{:S(2)}) collective-permute-start(s32[1,192]{1,0:T(1,128)S(1)} %collective-permute-done.1.target_one), channel_id=1, source_target_pairs={{0,8},{1,5},{2,10},{3,7},{8,16},{9,1},{10,18},{11,3},{16,24},{17,9... | collective-permute-start | bytes 2312 | tf_op jit(solution)/shard_map/ppermute | solution.py:366
  28.0 0.2 collective-permute-done.5.target_two
  28.2 0.2 collective-permute-done.4.two
  28.5 18.0 %shard_map.103.refs_0_ = f32[8,384]{1,0:T(8,128)S(1)} custom-call(s32[2]{0:T(128)S(1)} %pad_add_fusion.place, bf16[192,4096]{1,0:T(8,128)(2,1)} %collective-permute-done.one, bf16[192,4096]{1,0:T(8,128)(2,1)S(1)} %collective-permute-done.4.two, s32[1,192]{1,0:T(1,128)S(1)} %collective-permute-done.1.target_one, ...), custom_call_target="tpu_custom_call" | custom-call | flops 12608077824 | bytes 32833536 | tf_op jit(solution)/shard_map/pallas_call | solution.py:338
  46.5 0.0 collective-permute-done.3.target_one
  46.5 0.0 collective-permute-done.2.one
  46.5 0.2 collective-permute-start.8
  46.7 1.6 %collective-permute-start.6 = (bf16[192,4096]{1,0:T(8,128)(2,1)S(1)}, bf16[192,4096]{1,0:T(8,128)(2,1)S(1)}, u32[]{:S(2)}, u32[]{:S(2)}) collective-permute-start(bf16[192,4096]{1,0:T(8,128)(2,1)S(1)} %collective-permute-done.2.one), channel_id=1, source_target_pairs={{0,8},{1,5},{2,10},{3,7},{8,16},{9,1},{10,18},{11,3},{16,24},{17,9... | collective-permute-start | bytes 4718600 | tf_op jit(solution)/shard_map/ppermute | solution.py:366
  48.3 0.0 collective-permute-start.9
  48.3 1.5 %collective-permute-start.7 = (s32[1,192]{1,0:T(1,128)S(1)}, s32[1,192]{1,0:T(1,128)S(1)}, u32[]{:S(2)}, u32[]{:S(2)}) collective-permute-start(s32[1,192]{1,0:T(1,128)S(1)} %collective-permute-done.3.target_one), channel_id=1, source_target_pairs={{0,8},{1,5},{2,10},{3,7},{8,16},{9,1},{10,18},{11,3},{16,24},{17,9... | collective-permute-start | bytes 2312 | tf_op jit(solution)/shard_map/ppermute | solution.py:366
  49.8 0.2 collective-permute-done.9.target_two
  50.0 0.0 collective-permute-done.8.two
  50.0 17.2 %shard_map.104.refs_1_ = f32[8,384]{1,0:T(8,128)S(1)} custom-call(s32[2]{0:T(128)S(1)} %pad_add_fusion.place, bf16[192,4096]{1,0:T(8,128)(2,1)S(1)} %collective-permute-done.2.one, bf16[192,4096]{1,0:T(8,128)(2,1)S(1)} %collective-permute-done.8.two, s32[1,192]{1,0:T(1,128)S(1)} %collective-permute-done.3.target_one, ...), custom_call_target="tpu_custom_call" | custom-call | flops 12608077824 | bytes 32833536 | tf_op jit(solution)/shard_map/pallas_call | solution.py:338
  67.1 0.0 collective-permute-done.7.target.target_one
  67.2 0.0 collective-permute-done.6.block.one
  67.2 0.2 collective-permute-start.12
  67.3 0.4 collective-permute-start.13
  67.7 0.6 shard_map.105
  68.3 1.6 %collective-permute-start.10 = (bf16[96,4096]{1,0:T(8,128)(2,1)S(1)}, bf16[96,4096]{1,0:T(8,128)(2,1)S(1)}, u32[]{:S(2)}, u32[]{:S(2)}) collective-permute-start(bf16[96,4096]{1,0:T(8,128)(2,1)S(1)} %get-tuple-element.43), channel_id=1, source_target_pairs={{0,8},{1,5},{2,10},{3,7},{8,16},{9,1},{10,18},{11,3},{16,24},{17,9... | collective-permute-start | bytes 2359304 | tf_op jit(solution)/shard_map/ppermute | solution.py:366
  69.9 1.5 %collective-permute-start.11 = (s32[1,96]{1,0:T(1,128)S(1)}, s32[1,96]{1,0:T(1,128)S(1)}, u32[]{:S(2)}, u32[]{:S(2)}) collective-permute-start(s32[1,96]{1,0:T(1,128)S(1)} %get-tuple-element.44), channel_id=1, source_target_pairs={{0,8},{1,5},{2,10},{3,7},{8,16},{9,1},{10,18},{11,3},{16,24},{17,9... | collective-permute-start | bytes 1160 | tf_op jit(solution)/shard_map/ppermute | solution.py:366
  71.4 0.0 collective-permute-done.13.target_two
  71.4 0.0 collective-permute-done.12.two
  71.5 14.5 %shard_map.106.refs_2_ = f32[8,384]{1,0:T(8,128)S(1)} custom-call(s32[2]{0:T(128)S(1)} %pad_add_fusion.place, bf16[192,4096]{1,0:T(8,128)(2,1)S(1)} %collective-permute-done.6.block.one, bf16[192,4096]{1,0:T(8,128)(2,1)S(1)} %collective-permute-done.12.two, s32[1,192]{1,0:T(1,128)S(1)} %collective-permute-done.7.target.target_one, ...), custom_call_target="tpu_custom_call" | custom-call | flops 12608077824 | bytes 32833536 | tf_op jit(solution)/shard_map/pallas_call | solution.py:338
  85.9 0.0 collective-permute-done.11.target_one
  85.9 0.0 collective-permute-done.10.one
  85.9 0.1 collective-permute-start.15
  86.0 0.5 collective-permute-start.16
  86.5 0.7 shard_map.107
  87.2 0.0 copy-start.5
  87.2 0.1 collective-permute-start.14
  87.3 0.9 collective-permute-done.16.target_two
  88.3 0.0 collective-permute-done.15.two
  88.3 12.1 %shard_map.108.last = f32[8,256]{1,0:T(8,128)S(1)} custom-call(s32[2]{0:T(128)S(1)} %pad_add_fusion.place, bf16[96,4096]{1,0:T(8,128)(2,1)S(1)} %collective-permute-done.10.one, bf16[96,4096]{1,0:T(8,128)(2,1)S(1)} %collective-permute-done.15.two, s32[1,96]{1,0:T(1,128)S(1)} %collective-permute-done.11.target_one, ...), custom_call_target="tpu_custom_call" | custom-call | flops 6304038912 | bytes 32833536 | tf_op jit(solution)/shard_map/pallas_call | solution.py:338
  100.4 0.0 collective-permute-done.14.got
  100.4 0.6 shard_map.109
  101.1 13.4 %all_to_all.5.stats = f32[32,8,256]{2,1,0:T(8,128)S(1)} all-to-all(f32[32,8,256]{2,1,0:T(8,128)S(1)} %shard_map.109), channel_id=1, replica_groups=mesh['dp'=8,'tensor'=4] {'dp','tensor'}, dimensions={0} | all-to-all | bytes 524288 | tf_op jit(solution)/shard_map/all_to_all | solution.py:397
  114.5 1.6 %shard_map.110 = (f32[1,48]{1,0:T(1,128)}, f32[1,8]{1,0:T(1,128)}, f32[1,64]{1,0:T(1,128)}, f32[1,16]{1,0:T(1,128)}) custom-call(s32[2]{0:T(128)S(1)} %pad_add_fusion.place, f32[32,8,256]{2,1,0:T(8,128)S(1)} %all_to_all.5.stats, s32[1,16]{1,0:T(1,128)S(1)} %bitcast.17), custom_call_target="tpu_custom_call" | custom-call | tf_op jit(solution)/shard_map/pallas_call | solution.py:399
  (9 shorter events, 0.0 us)
Async XLA Ops:
  0.6 24.1 %collective-permute-start = (bf16[192,4096]{1,0:T(8,128)(2,1)}, bf16[192,4096]{1,0:T(8,128)(2,1)}, u32[]{:S(2)}, u32[]{:S(2)}) collective-permute-start(bf16[192,4096]{1,0:T(8,128)(2,1)} %rows.1), channel_id=1, source_target_pairs={{0,8},{1,5},{2,10},{3,7},{8,16},{9,1},{10,18},{11,3},{16,24},{17,9... | collective-permute-start | bytes 4718600 | tf_op jit(solution)/shard_map/ppermute | solution.py:366
  3.7 21.0 %collective-permute-start.1 = (s32[1,192]{1,0:T(1,128)}, s32[1,192]{1,0:T(1,128)S(1)}, u32[]{:S(2)}, u32[]{:S(2)}) collective-permute-start(s32[1,192]{1,0:T(1,128)} %bitcast.13), channel_id=1, source_target_pairs={{0,8},{1,5},{2,10},{3,7},{8,16},{9,1},{10,18},{11,3},{16,24},{17,9... | collective-permute-start | bytes 2312 | tf_op jit(solution)/shard_map/ppermute | solution.py:366
  5.4 1.4 %copy-start = (bf16[192,4096]{1,0:T(8,128)(2,1)S(1)}, bf16[192,4096]{1,0:T(8,128)(2,1)}, u32[]{:S(2)}) copy-start(bf16[192,4096]{1,0:T(8,128)(2,1)} %rows.1) | copy-start | bytes 4718596
  6.8 0.7 copy-start.2
  24.8 3.7 %collective-permute-start.4 = (bf16[192,4096]{1,0:T(8,128)(2,1)}, bf16[192,4096]{1,0:T(8,128)(2,1)S(1)}, u32[]{:S(2)}, u32[]{:S(2)}) collective-permute-start(bf16[192,4096]{1,0:T(8,128)(2,1)} %collective-permute-done.one), channel_id=1, source_target_pairs={{0,1},{1,0},{2,3},{3,2},{4,5},{5,4},{6,7},{7,6},{8,9},{9,8},{10,11... | collective-permute-start | bytes 4718600 | tf_op jit(solution)/shard_map/ppermute | solution.py:366
  24.8 21.6 %collective-permute-start.2 = (bf16[192,4096]{1,0:T(8,128)(2,1)}, bf16[192,4096]{1,0:T(8,128)(2,1)S(1)}, u32[]{:S(2)}, u32[]{:S(2)}) collective-permute-start(bf16[192,4096]{1,0:T(8,128)(2,1)} %collective-permute-done.one), channel_id=1, source_target_pairs={{0,8},{1,5},{2,10},{3,7},{8,16},{9,1},{10,18},{11,3},{16,24},{17,9... | collective-permute-start | bytes 4718600 | tf_op jit(solution)/shard_map/ppermute | solution.py:366
  26.5 1.7 %collective-permute-start.5 = (s32[1,192]{1,0:T(1,128)S(1)}, s32[1,192]{1,0:T(1,128)S(1)}, u32[]{:S(2)}, u32[]{:S(2)}) collective-permute-start(s32[1,192]{1,0:T(1,128)S(1)} %collective-permute-done.1.target_one), channel_id=1, source_target_pairs={{0,1},{1,0},{2,3},{3,2},{4,5},{5,4},{6,7},{7,6},{8,9},{9,8},{10,11... | collective-permute-start | bytes 2312 | tf_op jit(solution)/shard_map/ppermute | solution.py:366
  26.5 20.0 %collective-permute-start.3 = (s32[1,192]{1,0:T(1,128)S(1)}, s32[1,192]{1,0:T(1,128)S(1)}, u32[]{:S(2)}, u32[]{:S(2)}) collective-permute-start(s32[1,192]{1,0:T(1,128)S(1)} %collective-permute-done.1.target_one), channel_id=1, source_target_pairs={{0,8},{1,5},{2,10},{3,7},{8,16},{9,1},{10,18},{11,3},{16,24},{17,9... | collective-permute-start | bytes 2312 | tf_op jit(solution)/shard_map/ppermute | solution.py:366
  46.5 3.5 %collective-permute-start.8 = (bf16[192,4096]{1,0:T(8,128)(2,1)S(1)}, bf16[192,4096]{1,0:T(8,128)(2,1)S(1)}, u32[]{:S(2)}, u32[]{:S(2)}) collective-permute-start(bf16[192,4096]{1,0:T(8,128)(2,1)S(1)} %collective-permute-done.2.one), channel_id=1, source_target_pairs={{0,1},{1,0},{2,3},{3,2},{4,5},{5,4},{6,7},{7,6},{8,9},{9,8},{10,11... | collective-permute-start | bytes 4718600 | tf_op jit(solution)/shard_map/ppermute | solution.py:366
  46.7 20.5 %collective-permute-start.6 = (bf16[192,4096]{1,0:T(8,128)(2,1)S(1)}, bf16[192,4096]{1,0:T(8,128)(2,1)S(1)}, u32[]{:S(2)}, u32[]{:S(2)}) collective-permute-start(bf16[192,4096]{1,0:T(8,128)(2,1)S(1)} %collective-permute-done.2.one), channel_id=1, source_target_pairs={{0,8},{1,5},{2,10},{3,7},{8,16},{9,1},{10,18},{11,3},{16,24},{17,9... | collective-permute-start | bytes 4718600 | tf_op jit(solution)/shard_map/ppermute | solution.py:366
  48.3 1.7 %collective-permute-start.9 = (s32[1,192]{1,0:T(1,128)S(1)}, s32[1,192]{1,0:T(1,128)S(1)}, u32[]{:S(2)}, u32[]{:S(2)}) collective-permute-start(s32[1,192]{1,0:T(1,128)S(1)} %collective-permute-done.3.target_one), channel_id=1, source_target_pairs={{0,1},{1,0},{2,3},{3,2},{4,5},{5,4},{6,7},{7,6},{8,9},{9,8},{10,11... | collective-permute-start | bytes 2312 | tf_op jit(solution)/shard_map/ppermute | solution.py:366
  48.3 18.9 %collective-permute-start.7 = (s32[1,192]{1,0:T(1,128)S(1)}, s32[1,192]{1,0:T(1,128)S(1)}, u32[]{:S(2)}, u32[]{:S(2)}) collective-permute-start(s32[1,192]{1,0:T(1,128)S(1)} %collective-permute-done.3.target_one), channel_id=1, source_target_pairs={{0,8},{1,5},{2,10},{3,7},{8,16},{9,1},{10,18},{11,3},{16,24},{17,9... | collective-permute-start | bytes 2312 | tf_op jit(solution)/shard_map/ppermute | solution.py:366
  67.2 4.3 %collective-permute-start.12 = (bf16[192,4096]{1,0:T(8,128)(2,1)S(1)}, bf16[192,4096]{1,0:T(8,128)(2,1)S(1)}, u32[]{:S(2)}, u32[]{:S(2)}) collective-permute-start(bf16[192,4096]{1,0:T(8,128)(2,1)S(1)} %collective-permute-done.6.block.one), channel_id=1, source_target_pairs={{0,1},{1,0},{2,3},{3,2},{4,5},{5,4},{6,7},{7,6},{8,9},{9,8},{10,11... | collective-permute-start | bytes 4718600 | tf_op jit(solution)/shard_map/ppermute | solution.py:366
  67.3 4.1 %collective-permute-start.13 = (s32[1,192]{1,0:T(1,128)S(1)}, s32[1,192]{1,0:T(1,128)S(1)}, u32[]{:S(2)}, u32[]{:S(2)}) collective-permute-start(s32[1,192]{1,0:T(1,128)S(1)} %collective-permute-done.7.target.target_one), channel_id=1, source_target_pairs={{0,1},{1,0},{2,3},{3,2},{4,5},{5,4},{6,7},{7,6},{8,9},{9,8},{10,11... | collective-permute-start | bytes 2312 | tf_op jit(solution)/shard_map/ppermute | solution.py:366
  68.3 17.6 %collective-permute-start.10 = (bf16[96,4096]{1,0:T(8,128)(2,1)S(1)}, bf16[96,4096]{1,0:T(8,128)(2,1)S(1)}, u32[]{:S(2)}, u32[]{:S(2)}) collective-permute-start(bf16[96,4096]{1,0:T(8,128)(2,1)S(1)} %get-tuple-element.43), channel_id=1, source_target_pairs={{0,8},{1,5},{2,10},{3,7},{8,16},{9,1},{10,18},{11,3},{16,24},{17,9... | collective-permute-start | bytes 2359304 | tf_op jit(solution)/shard_map/ppermute | solution.py:366
  69.9 16.0 %collective-permute-start.11 = (s32[1,96]{1,0:T(1,128)S(1)}, s32[1,96]{1,0:T(1,128)S(1)}, u32[]{:S(2)}, u32[]{:S(2)}) collective-permute-start(s32[1,96]{1,0:T(1,128)S(1)} %get-tuple-element.44), channel_id=1, source_target_pairs={{0,8},{1,5},{2,10},{3,7},{8,16},{9,1},{10,18},{11,3},{16,24},{17,9... | collective-permute-start | bytes 1160 | tf_op jit(solution)/shard_map/ppermute | solution.py:366
  85.9 2.3 %collective-permute-start.15 = (bf16[96,4096]{1,0:T(8,128)(2,1)S(1)}, bf16[96,4096]{1,0:T(8,128)(2,1)S(1)}, u32[]{:S(2)}, u32[]{:S(2)}) collective-permute-start(bf16[96,4096]{1,0:T(8,128)(2,1)S(1)} %collective-permute-done.10.one), channel_id=1, source_target_pairs={{0,1},{1,0},{2,3},{3,2},{4,5},{5,4},{6,7},{7,6},{8,9},{9,8},{10,11... | collective-permute-start | bytes 2359304 | tf_op jit(solution)/shard_map/ppermute | solution.py:366
  86.0 2.3 %collective-permute-start.16 = (s32[1,96]{1,0:T(1,128)S(1)}, s32[1,96]{1,0:T(1,128)S(1)}, u32[]{:S(2)}, u32[]{:S(2)}) collective-permute-start(s32[1,96]{1,0:T(1,128)S(1)} %collective-permute-done.11.target_one), channel_id=1, source_target_pairs={{0,1},{1,0},{2,3},{3,2},{4,5},{5,4},{6,7},{7,6},{8,9},{9,8},{10,11... | collective-permute-start | bytes 1160 | tf_op jit(solution)/shard_map/ppermute | solution.py:366
  87.2 13.3 %copy-start.1 = (s32[192,1]{0,1:T(1,128)S(1)}, s32[192,1]{0,1:T(1,128)}, u32[]{:S(2)}) copy-start(s32[192,1]{0,1:T(1,128)} %param.10) | copy-start | bytes 2308
  87.2 13.3 %copy-start.3 = (f32[8]{0:T(128)S(1)}, f32[8]{0:T(128)}, u32[]{:S(2)}) copy-start(f32[8]{0:T(128)} %param.11) | copy-start | bytes 100
  87.2 13.3 %copy-start.4 = (f32[8]{0:T(128)S(1)}, f32[8]{0:T(128)}, u32[]{:S(2)}) copy-start(f32[8]{0:T(128)} %param.12) | copy-start | bytes 100
  87.2 27.3 %copy-start.5 = (s32[16]{0:T(128)S(1)}, s32[16]{0:T(128)}, u32[]{:S(2)}) copy-start(s32[16]{0:T(128)} %param.13) | copy-start | bytes 196
  87.2 13.2 %collective-permute-start.14 = (f32[8,256]{1,0:T(8,128)S(1)}, f32[8,256]{1,0:T(8,128)S(1)}, u32[]{:S(2)}, u32[]{:S(2)}) collective-permute-start(f32[8,256]{1,0:T(8,128)S(1)} %get-tuple-element.47), channel_id=1, source_target_pairs={{0,1},{1,0},{2,3},{3,2},{4,5},{5,4},{6,7},{7,6},{8,9},{9,8},{10,11... | collective-permute-start | bytes 24584 | tf_op jit(solution)/shard_map/ppermute | solution.py:366
where the time goes:
time: 116 us
  Pallas kernels  82.6 us (71%)
  starting transfers between devices  15.6 us (13%)
  blocking collectives  13.4 us (12%)
  local copies, waits for them, and re-layouts  2.1 us (2%)
  waiting for transfers between devices  1.62 us (1%)
    pallas_call x5, Pallas kernels, stats_of(): pl.pallas_call(functools.partial(first_kernel, tensor_count) if first els...  79.1 us
    ppermute x17, starting transfers between devices, moved(): return [lax.ppermute(x, axes, way) for x in arrays]  15.6 us
    all_to_all x1, blocking collectives, body(): every = lax.all_to_all(table, AXES, split_axis=0, concat_axis=0, tiled=True)  13.4 us
  transfers between devices with their start and end apart: 17, of which 4 were waited for; matrix products, arithmetic and copies ran while one was open for 0% of the time, Pallas kernels for 69%

commit v1 on v0

--- a/solution.py
+++ b/solution.py
@@ -35,19 +35,18 @@
 
 
 def each_tile(groups, limit, visit):
-    number = 0
-    for place, group in enumerate(groups):
+    for place, group in reversed(list(enumerate(groups))):
+        number = place * GROUP
         count = group.shape[0] // TILE
         turn = limit if count % limit == 0 else count
 
-        def body(i, carry, group=group, number=number, turn=turn, final=place == len(groups) - 1):
+        def body(i, carry, group=group, number=number, count=count, turn=turn, final=place == len(groups) - 1):
             for j in range(turn):
-                tile = i * turn + j
+                tile = count - 1 - (i * turn + j)
                 visit(group.at[pl.ds(pl.multiple_of(tile * TILE, TILE), TILE), :], number + tile, final)
             return carry
 
         lax.fori_loop(0, count // turn, body, 0)
-        number += count
 
 
 def slice_stats(rows, walk, vocab, wanted, vocab_offset, top, total, picked):
@@ -60,10 +59,11 @@
 
     def visit(weights, tile, final):
         logits = lax.dot_general(rows, weights[...], NT, preferred_element_type=jnp.float32)
-        start = tile * TILE
+        size = weights.shape[0]
+        start = tile * size
         parts = []
         chosen = picked[...]
-        for i in range(0, TILE, 128):
+        for i in range(0, size, 128):
             part = logits[:, i : i + 128]
             found = wanted == start + i
             if final:
@@ -101,7 +101,8 @@
 
     def visit(weights, tile, final):
         logits = lax.dot_general(weights[...], rows, NT, preferred_element_type=jnp.float32)
-        start = tile * TILE
+        size = weights.shape[0]
+        start = tile * size
         number = lax.broadcasted_iota(jnp.int32, logits.shape, 0)
         if final:
             logits = jnp.where(number < vocab - start, logits, LOW)
@@ -109,8 +110,8 @@
         if final:
             found = found & (number < vocab - start)
         found = jnp.where(found, logits, 0.0)
-        logits = logits.reshape(TILE // 8, 8, count)
-        picked[...] += jnp.sum(found.reshape(TILE // 8, 8, count), axis=0)
+        logits = logits.reshape(size // 8, 8, count)
+        picked[...] += jnp.sum(found.reshape(size // 8, 8, count), axis=0)
         before = top[...]
         now = jnp.maximum(before, jnp.max(logits, axis=0))
         total[...] = total[...] * jnp.exp(before - now) + jnp.sum(jnp.exp(logits - now[None]), axis=0)
@@ -140,7 +141,7 @@
     copies = [
         pltpu.make_async_copy(weight.at[pl.ds(i * TILE, TILE), :], tiles[i], arrived.at[i]) for i in range(last)
     ]
-    for copy in copies:
+    for copy in reversed(copies):
         copy.start()
     tiles[last][...] = ending[...]
 
@@ -150,12 +151,21 @@
             def _():
                 pltpu.make_async_copy(tiles[0], tiles[0], arrived.at[tile]).wait()
 
-            visit(weights, tile, final)
+            def half(i, carry):
+                visit(weights.at[pl.ds(pl.multiple_of(i * (TILE // 2), TILE // 2), TILE // 2), :], 2 * tile + i, final)
+                return carry
+
+            lax.fori_loop(0, 2, half, 0)
 
         each_tile(groups, 1, arriving)
 
-    wanted = column_from(target[...])
-    out[...] = slice_stats(rows[...], walk, vocab, wanted, offset_of(place, tensor_count, vocab), *scratch)
+    offset = offset_of(place, tensor_count, vocab)
+    if rows.shape[0] > FEW:
+        out[...] = slice_stats(rows[...], walk, vocab, column_from(target[...]), offset, *scratch)
+    else:
+        logs, picks = few_stats(rows[...], walk, vocab, target[...], offset, *scratch)
+        out[0:1, : rows.shape[0]] = logs
+        out[1:2, : rows.shape[0]] = picks
 
 
 def pair_kernel(tensor_count, vocab, turn, place, one, two, target_one, target_two, *rest):
@@ -334,7 +344,7 @@
         rows = sum(block.shape[0] for block in blocks)
         first = not kept
         table = jax.ShapeDtypeStruct((8, up_to(rows, 128)), jnp.float32)
-        sums = pltpu.VMEM((rows, 128) if first or rows > FEW else (8, rows), jnp.float32)
+        sums = pltpu.VMEM((rows, 128) if rows > FEW else (8, rows), jnp.float32)
         return pl.pallas_call(
             functools.partial(first_kernel, tensor_count) if first else functools.partial(pair_kernel, tensor_count, vocab, turn),
             grid=(1,),
@@ -384,7 +394,7 @@
                 compiler_params=limit,
             )(place, *gathered)
             [got] = moved("tensor", across, theirs)
-        gathered.append(stats_of([block, other], [wanted, wanted_other], kept, GROUP if step == steps else 1))
+        gathered.append(stats_of([block, other], [wanted, wanted_other], kept, GROUP if step >= steps else 1))
 
     table = pl.pallas_call(
         functools.partial(pack_kernel, size, steps),

time: 116 us -> 115 us (level)
  Pallas kernels: 82.6 us -> 79.1 us
  blocking collectives: 13.4 us -> 15.1 us
    pallas_call x5, Pallas kernels: 79.1 us -> 75.6 us  [stats_of(): pl.pallas_call(functools.partial(first_kernel, tensor_count) if first els...]
    all_to_all x1, blocking collectives: 13.4 us -> 15.1 us  [body(): every = lax.all_to_all(table, AXES, split_axis=0, concat_axis=0, tiled=True)]
  transfers between devices with their start and end apart: 17 -> 17, of which waited for: 4 -> 5; matrix products, arithmetic and copies ran while one was open for 0% -> 0% of each run, Pallas kernels for 69% -> 67%
where the time goes in v1:
time: 115 us; the launch traced here: 114 us
  Pallas kernels  79.1 us (69%)
  starting transfers between devices  15.6 us (14%)
  blocking collectives  15.1 us (13%)
  local copies, waits for them, and re-layouts  2.1 us (2%)
  waiting for transfers between devices  1.64 us (1%)
    pallas_call x5, Pallas kernels, stats_of(): pl.pallas_call(functools.partial(first_kernel, tensor_count) if first els...  75.6 us
    ppermute x17, starting transfers between devices, moved(): return [lax.ppermute(x, axes, way) for x in arrays]  15.6 us
    all_to_all x1, blocking collectives, body(): every = lax.all_to_all(table, AXES, split_axis=0, concat_axis=0, tiled=True)  15.1 us
  transfers between devices with their start and end apart: 17, of which 5 were waited for; matrix products, arithmetic and copies ran while one was open for 0% of the time, Pallas kernels for 67%

profile of v1, /device:TPU:0, one launch (start us, length us, event | category | flops | bytes accessed | tf_op | source)
XLA Modules:
  0.0 114.3 jit_solution(8386532974697021750)
XLA Ops:
  0.6 3.1 %collective-permute-start = (bf16[192,4096]{1,0:T(8,128)(2,1)}, bf16[192,4096]{1,0:T(8,128)(2,1)}, u32[]{:S(2)}, u32[]{:S(2)}) collective-permute-start(bf16[192,4096]{1,0:T(8,128)(2,1)} %rows.1), channel_id=1, source_target_pairs={{0,8},{1,5},{2,10},{3,7},{8,16},{9,1},{10,18},{11,3},{16,24},{17,9... | collective-permute-start | bytes 4718600 | tf_op jit(solution)/shard_map/ppermute | solution.py:376
  3.7 1.6 %collective-permute-start.1 = (s32[1,192]{1,0:T(1,128)}, s32[1,192]{1,0:T(1,128)S(1)}, u32[]{:S(2)}, u32[]{:S(2)}) collective-permute-start(s32[1,192]{1,0:T(1,128)} %bitcast.13), channel_id=1, source_target_pairs={{0,8},{1,5},{2,10},{3,7},{8,16},{9,1},{10,18},{11,3},{16,24},{17,9... | collective-permute-start | bytes 2312 | tf_op jit(solution)/shard_map/ppermute | solution.py:376
  5.3 0.1 pad_add_fusion.place
  5.4 1.4 %copy-done = bf16[192,4096]{1,0:T(8,128)(2,1)S(1)} copy-done((bf16[192,4096]{1,0:T(8,128)(2,1)S(1)}, bf16[192,4096]{1,0:T(8,128)(2,1)}, u32[]{:S(2)}) %copy-start) | copy-done | bytes 1572888
  6.8 0.7 copy-done.2
  7.4 15.6 %shard_map.102 = (f32[8,256]{1,0:T(8,128)S(1)}, bf16[1024,4096]{1,0:T(8,128)(2,1)S(1)}, bf16[1024,4096]{1,0:T(8,128)(2,1)S(1)}, bf16[1024,4096]{1,0:T(8,128)(2,1)S(1)}, bf16[1024,4096]{1,0:T(8,128)(2,1)S(1)}) custom-call(s32[2]{0:T(128)S(1)} %pad_add_fusion.place, bf16[192,4096]{1,0:T(8,128)(2,1)S(1)} %copy-done, s32[1,192]{1,0:T(1,128)S(1)} %bitcast.14, ...), custom_call_target="tpu_custom_call" | custom-call | flops 6304038912 | bytes 32833536 | tf_op jit(solution)/shard_map/pallas_call | solution.py:348
  23.0 0.0 collective-permute-done.1.target_one
  23.1 0.0 collective-permute-done.one
  23.1 0.1 collective-permute-start.4
  23.1 1.6 %collective-permute-start.2 = (bf16[192,4096]{1,0:T(8,128)(2,1)}, bf16[192,4096]{1,0:T(8,128)(2,1)S(1)}, u32[]{:S(2)}, u32[]{:S(2)}) collective-permute-start(bf16[192,4096]{1,0:T(8,128)(2,1)} %collective-permute-done.one), channel_id=1, source_target_pairs={{0,8},{1,5},{2,10},{3,7},{8,16},{9,1},{10,18},{11,3},{16,24},{17,9... | collective-permute-start | bytes 4718600 | tf_op jit(solution)/shard_map/ppermute | solution.py:376
  24.8 0.0 collective-permute-start.5
  24.8 1.5 %collective-permute-start.3 = (s32[1,192]{1,0:T(1,128)S(1)}, s32[1,192]{1,0:T(1,128)S(1)}, u32[]{:S(2)}, u32[]{:S(2)}) collective-permute-start(s32[1,192]{1,0:T(1,128)S(1)} %collective-permute-done.1.target_one), channel_id=1, source_target_pairs={{0,8},{1,5},{2,10},{3,7},{8,16},{9,1},{10,18},{11,3},{16,24},{17,9... | collective-permute-start | bytes 2312 | tf_op jit(solution)/shard_map/ppermute | solution.py:376
  26.3 0.2 collective-permute-done.5.target_two
  26.5 0.2 collective-permute-done.4.two
  26.8 18.0 %shard_map.103.refs_0_ = f32[8,384]{1,0:T(8,128)S(1)} custom-call(s32[2]{0:T(128)S(1)} %pad_add_fusion.place, bf16[192,4096]{1,0:T(8,128)(2,1)} %collective-permute-done.one, bf16[192,4096]{1,0:T(8,128)(2,1)S(1)} %collective-permute-done.4.two, s32[1,192]{1,0:T(1,128)S(1)} %collective-permute-done.1.target_one, ...), custom_call_target="tpu_custom_call" | custom-call | flops 12608077824 | bytes 32833536 | tf_op jit(solution)/shard_map/pallas_call | solution.py:348
  44.8 0.0 collective-permute-done.3.target_one
  44.8 0.0 collective-permute-done.2.one
  44.8 0.2 collective-permute-start.8
  45.0 1.6 %collective-permute-start.6 = (bf16[192,4096]{1,0:T(8,128)(2,1)S(1)}, bf16[192,4096]{1,0:T(8,128)(2,1)S(1)}, u32[]{:S(2)}, u32[]{:S(2)}) collective-permute-start(bf16[192,4096]{1,0:T(8,128)(2,1)S(1)} %collective-permute-done.2.one), channel_id=1, source_target_pairs={{0,8},{1,5},{2,10},{3,7},{8,16},{9,1},{10,18},{11,3},{16,24},{17,9... | collective-permute-start | bytes 4718600 | tf_op jit(solution)/shard_map/ppermute | solution.py:376
  46.6 0.0 collective-permute-start.9
  46.6 1.5 %collective-permute-start.7 = (s32[1,192]{1,0:T(1,128)S(1)}, s32[1,192]{1,0:T(1,128)S(1)}, u32[]{:S(2)}, u32[]{:S(2)}) collective-permute-start(s32[1,192]{1,0:T(1,128)S(1)} %collective-permute-done.3.target_one), channel_id=1, source_target_pairs={{0,8},{1,5},{2,10},{3,7},{8,16},{9,1},{10,18},{11,3},{16,24},{17,9... | collective-permute-start | bytes 2312 | tf_op jit(solution)/shard_map/ppermute | solution.py:376
  48.1 0.2 collective-permute-done.9.target_two
  48.2 0.0 collective-permute-done.8.two
  48.3 17.1 %shard_map.104.refs_1_ = f32[8,384]{1,0:T(8,128)S(1)} custom-call(s32[2]{0:T(128)S(1)} %pad_add_fusion.place, bf16[192,4096]{1,0:T(8,128)(2,1)S(1)} %collective-permute-done.2.one, bf16[192,4096]{1,0:T(8,128)(2,1)S(1)} %collective-permute-done.8.two, s32[1,192]{1,0:T(1,128)S(1)} %collective-permute-done.3.target_one, ...), custom_call_target="tpu_custom_call" | custom-call | flops 12608077824 | bytes 32833536 | tf_op jit(solution)/shard_map/pallas_call | solution.py:348
  65.4 0.1 collective-permute-done.7.target.target_one
  65.4 0.0 collective-permute-done.6.block.one
  65.4 0.1 collective-permute-start.12
  65.6 0.4 collective-permute-start.13
  66.0 0.6 shard_map.105
  66.6 1.6 %collective-permute-start.10 = (bf16[96,4096]{1,0:T(8,128)(2,1)S(1)}, bf16[96,4096]{1,0:T(8,128)(2,1)S(1)}, u32[]{:S(2)}, u32[]{:S(2)}) collective-permute-start(bf16[96,4096]{1,0:T(8,128)(2,1)S(1)} %get-tuple-element.43), channel_id=1, source_target_pairs={{0,8},{1,5},{2,10},{3,7},{8,16},{9,1},{10,18},{11,3},{16,24},{17,9... | collective-permute-start | bytes 2359304 | tf_op jit(solution)/shard_map/ppermute | solution.py:376
  68.2 1.5 %collective-permute-start.11 = (s32[1,96]{1,0:T(1,128)S(1)}, s32[1,96]{1,0:T(1,128)S(1)}, u32[]{:S(2)}, u32[]{:S(2)}) collective-permute-start(s32[1,96]{1,0:T(1,128)S(1)} %get-tuple-element.44), channel_id=1, source_target_pairs={{0,8},{1,5},{2,10},{3,7},{8,16},{9,1},{10,18},{11,3},{16,24},{17,9... | collective-permute-start | bytes 1160 | tf_op jit(solution)/shard_map/ppermute | solution.py:376
  69.7 0.0 collective-permute-done.13.target_two
  69.7 0.0 collective-permute-done.12.two
  69.7 14.4 %shard_map.106.refs_2_ = f32[8,384]{1,0:T(8,128)S(1)} custom-call(s32[2]{0:T(128)S(1)} %pad_add_fusion.place, bf16[192,4096]{1,0:T(8,128)(2,1)S(1)} %collective-permute-done.6.block.one, bf16[192,4096]{1,0:T(8,128)(2,1)S(1)} %collective-permute-done.12.two, s32[1,192]{1,0:T(1,128)S(1)} %collective-permute-done.7.target.target_one, ...), custom_call_target="tpu_custom_call" | custom-call | flops 12608077824 | bytes 32833536 | tf_op jit(solution)/shard_map/pallas_call | solution.py:348
  84.2 0.0 collective-permute-done.11.target_one
  84.2 0.0 collective-permute-done.10.one
  84.2 0.1 collective-permute-start.15
  84.2 0.5 collective-permute-start.16
  84.7 0.7 shard_map.107
  85.4 0.0 copy-start.5
  85.5 0.1 collective-permute-start.14
  85.6 0.9 collective-permute-done.16.target_two
  86.5 0.0 collective-permute-done.15.two
  86.5 10.4 %shard_map.108.last = f32[8,256]{1,0:T(8,128)S(1)} custom-call(s32[2]{0:T(128)S(1)} %pad_add_fusion.place, bf16[96,4096]{1,0:T(8,128)(2,1)S(1)} %collective-permute-done.10.one, bf16[96,4096]{1,0:T(8,128)(2,1)S(1)} %collective-permute-done.15.two, s32[1,96]{1,0:T(1,128)S(1)} %collective-permute-done.11.target_one, ...), custom_call_target="tpu_custom_call" | custom-call | flops 6304038912 | bytes 32833536 | tf_op jit(solution)/shard_map/pallas_call | solution.py:348
  96.9 0.0 collective-permute-done.14.got
  97.0 0.6 shard_map.109
  97.6 15.1 %all_to_all.5.stats = f32[32,8,256]{2,1,0:T(8,128)S(1)} all-to-all(f32[32,8,256]{2,1,0:T(8,128)S(1)} %shard_map.109), channel_id=1, replica_groups=mesh['dp'=8,'tensor'=4] {'dp','tensor'}, dimensions={0} | all-to-all | bytes 524288 | tf_op jit(solution)/shard_map/all_to_all | solution.py:407
  112.7 1.6 %shard_map.110 = (f32[1,48]{1,0:T(1,128)}, f32[1,8]{1,0:T(1,128)}, f32[1,64]{1,0:T(1,128)}, f32[1,16]{1,0:T(1,128)}) custom-call(s32[2]{0:T(128)S(1)} %pad_add_fusion.place, f32[32,8,256]{2,1,0:T(8,128)S(1)} %all_to_all.5.stats, s32[1,16]{1,0:T(1,128)S(1)} %bitcast.17), custom_call_target="tpu_custom_call" | custom-call | tf_op jit(solution)/shard_map/pallas_call | solution.py:409
  (9 shorter events, 0.0 us)
Async XLA Ops:
  0.6 22.4 %collective-permute-start = (bf16[192,4096]{1,0:T(8,128)(2,1)}, bf16[192,4096]{1,0:T(8,128)(2,1)}, u32[]{:S(2)}, u32[]{:S(2)}) collective-permute-start(bf16[192,4096]{1,0:T(8,128)(2,1)} %rows.1), channel_id=1, source_target_pairs={{0,8},{1,5},{2,10},{3,7},{8,16},{9,1},{10,18},{11,3},{16,24},{17,9... | collective-permute-start | bytes 4718600 | tf_op jit(solution)/shard_map/ppermute | solution.py:376
  3.7 19.3 %collective-permute-start.1 = (s32[1,192]{1,0:T(1,128)}, s32[1,192]{1,0:T(1,128)S(1)}, u32[]{:S(2)}, u32[]{:S(2)}) collective-permute-start(s32[1,192]{1,0:T(1,128)} %bitcast.13), channel_id=1, source_target_pairs={{0,8},{1,5},{2,10},{3,7},{8,16},{9,1},{10,18},{11,3},{16,24},{17,9... | collective-permute-start | bytes 2312 | tf_op jit(solution)/shard_map/ppermute | solution.py:376
  5.4 1.4 %copy-start = (bf16[192,4096]{1,0:T(8,128)(2,1)S(1)}, bf16[192,4096]{1,0:T(8,128)(2,1)}, u32[]{:S(2)}) copy-start(bf16[192,4096]{1,0:T(8,128)(2,1)} %rows.1) | copy-start | bytes 4718596
  6.8 0.7 copy-start.2
  23.1 3.7 %collective-permute-start.4 = (bf16[192,4096]{1,0:T(8,128)(2,1)}, bf16[192,4096]{1,0:T(8,128)(2,1)S(1)}, u32[]{:S(2)}, u32[]{:S(2)}) collective-permute-start(bf16[192,4096]{1,0:T(8,128)(2,1)} %collective-permute-done.one), channel_id=1, source_target_pairs={{0,1},{1,0},{2,3},{3,2},{4,5},{5,4},{6,7},{7,6},{8,9},{9,8},{10,11... | collective-permute-start | bytes 4718600 | tf_op jit(solution)/shard_map/ppermute | solution.py:376
  23.1 21.6 %collective-permute-start.2 = (bf16[192,4096]{1,0:T(8,128)(2,1)}, bf16[192,4096]{1,0:T(8,128)(2,1)S(1)}, u32[]{:S(2)}, u32[]{:S(2)}) collective-permute-start(bf16[192,4096]{1,0:T(8,128)(2,1)} %collective-permute-done.one), channel_id=1, source_target_pairs={{0,8},{1,5},{2,10},{3,7},{8,16},{9,1},{10,18},{11,3},{16,24},{17,9... | collective-permute-start | bytes 4718600 | tf_op jit(solution)/shard_map/ppermute | solution.py:376
  24.8 1.7 %collective-permute-start.5 = (s32[1,192]{1,0:T(1,128)S(1)}, s32[1,192]{1,0:T(1,128)S(1)}, u32[]{:S(2)}, u32[]{:S(2)}) collective-permute-start(s32[1,192]{1,0:T(1,128)S(1)} %collective-permute-done.1.target_one), channel_id=1, source_target_pairs={{0,1},{1,0},{2,3},{3,2},{4,5},{5,4},{6,7},{7,6},{8,9},{9,8},{10,11... | collective-permute-start | bytes 2312 | tf_op jit(solution)/shard_map/ppermute | solution.py:376
  24.8 20.0 %collective-permute-start.3 = (s32[1,192]{1,0:T(1,128)S(1)}, s32[1,192]{1,0:T(1,128)S(1)}, u32[]{:S(2)}, u32[]{:S(2)}) collective-permute-start(s32[1,192]{1,0:T(1,128)S(1)} %collective-permute-done.1.target_one), channel_id=1, source_target_pairs={{0,8},{1,5},{2,10},{3,7},{8,16},{9,1},{10,18},{11,3},{16,24},{17,9... | collective-permute-start | bytes 2312 | tf_op jit(solution)/shard_map/ppermute | solution.py:376
  44.8 3.5 %collective-permute-start.8 = (bf16[192,4096]{1,0:T(8,128)(2,1)S(1)}, bf16[192,4096]{1,0:T(8,128)(2,1)S(1)}, u32[]{:S(2)}, u32[]{:S(2)}) collective-permute-start(bf16[192,4096]{1,0:T(8,128)(2,1)S(1)} %collective-permute-done.2.one), channel_id=1, source_target_pairs={{0,1},{1,0},{2,3},{3,2},{4,5},{5,4},{6,7},{7,6},{8,9},{9,8},{10,11... | collective-permute-start | bytes 4718600 | tf_op jit(solution)/shard_map/ppermute | solution.py:376
  45.0 20.5 %collective-permute-start.6 = (bf16[192,4096]{1,0:T(8,128)(2,1)S(1)}, bf16[192,4096]{1,0:T(8,128)(2,1)S(1)}, u32[]{:S(2)}, u32[]{:S(2)}) collective-permute-start(bf16[192,4096]{1,0:T(8,128)(2,1)S(1)} %collective-permute-done.2.one), channel_id=1, source_target_pairs={{0,8},{1,5},{2,10},{3,7},{8,16},{9,1},{10,18},{11,3},{16,24},{17,9... | collective-permute-start | bytes 4718600 | tf_op jit(solution)/shard_map/ppermute | solution.py:376
  46.6 1.7 %collective-permute-start.9 = (s32[1,192]{1,0:T(1,128)S(1)}, s32[1,192]{1,0:T(1,128)S(1)}, u32[]{:S(2)}, u32[]{:S(2)}) collective-permute-start(s32[1,192]{1,0:T(1,128)S(1)} %collective-permute-done.3.target_one), channel_id=1, source_target_pairs={{0,1},{1,0},{2,3},{3,2},{4,5},{5,4},{6,7},{7,6},{8,9},{9,8},{10,11... | collective-permute-start | bytes 2312 | tf_op jit(solution)/shard_map/ppermute | solution.py:376
  46.6 18.9 %collective-permute-start.7 = (s32[1,192]{1,0:T(1,128)S(1)}, s32[1,192]{1,0:T(1,128)S(1)}, u32[]{:S(2)}, u32[]{:S(2)}) collective-permute-start(s32[1,192]{1,0:T(1,128)S(1)} %collective-permute-done.3.target_one), channel_id=1, source_target_pairs={{0,8},{1,5},{2,10},{3,7},{8,16},{9,1},{10,18},{11,3},{16,24},{17,9... | collective-permute-start | bytes 2312 | tf_op jit(solution)/shard_map/ppermute | solution.py:376
  65.4 4.3 %collective-permute-start.12 = (bf16[192,4096]{1,0:T(8,128)(2,1)S(1)}, bf16[192,4096]{1,0:T(8,128)(2,1)S(1)}, u32[]{:S(2)}, u32[]{:S(2)}) collective-permute-start(bf16[192,4096]{1,0:T(8,128)(2,1)S(1)} %collective-permute-done.6.block.one), channel_id=1, source_target_pairs={{0,1},{1,0},{2,3},{3,2},{4,5},{5,4},{6,7},{7,6},{8,9},{9,8},{10,11... | collective-permute-start | bytes 4718600 | tf_op jit(solution)/shard_map/ppermute | solution.py:376
  65.6 4.1 %collective-permute-start.13 = (s32[1,192]{1,0:T(1,128)S(1)}, s32[1,192]{1,0:T(1,128)S(1)}, u32[]{:S(2)}, u32[]{:S(2)}) collective-permute-start(s32[1,192]{1,0:T(1,128)S(1)} %collective-permute-done.7.target.target_one), channel_id=1, source_target_pairs={{0,1},{1,0},{2,3},{3,2},{4,5},{5,4},{6,7},{7,6},{8,9},{9,8},{10,11... | collective-permute-start | bytes 2312 | tf_op jit(solution)/shard_map/ppermute | solution.py:376
  66.6 17.6 %collective-permute-start.10 = (bf16[96,4096]{1,0:T(8,128)(2,1)S(1)}, bf16[96,4096]{1,0:T(8,128)(2,1)S(1)}, u32[]{:S(2)}, u32[]{:S(2)}) collective-permute-start(bf16[96,4096]{1,0:T(8,128)(2,1)S(1)} %get-tuple-element.43), channel_id=1, source_target_pairs={{0,8},{1,5},{2,10},{3,7},{8,16},{9,1},{10,18},{11,3},{16,24},{17,9... | collective-permute-start | bytes 2359304 | tf_op jit(solution)/shard_map/ppermute | solution.py:376
  68.2 16.0 %collective-permute-start.11 = (s32[1,96]{1,0:T(1,128)S(1)}, s32[1,96]{1,0:T(1,128)S(1)}, u32[]{:S(2)}, u32[]{:S(2)}) collective-permute-start(s32[1,96]{1,0:T(1,128)S(1)} %get-tuple-element.44), channel_id=1, source_target_pairs={{0,8},{1,5},{2,10},{3,7},{8,16},{9,1},{10,18},{11,3},{16,24},{17,9... | collective-permute-start | bytes 1160 | tf_op jit(solution)/shard_map/ppermute | solution.py:376
  84.2 2.3 %collective-permute-start.15 = (bf16[96,4096]{1,0:T(8,128)(2,1)S(1)}, bf16[96,4096]{1,0:T(8,128)(2,1)S(1)}, u32[]{:S(2)}, u32[]{:S(2)}) collective-permute-start(bf16[96,4096]{1,0:T(8,128)(2,1)S(1)} %collective-permute-done.10.one), channel_id=1, source_target_pairs={{0,1},{1,0},{2,3},{3,2},{4,5},{5,4},{6,7},{7,6},{8,9},{9,8},{10,11... | collective-permute-start | bytes 2359304 | tf_op jit(solution)/shard_map/ppermute | solution.py:376
  84.2 2.3 %collective-permute-start.16 = (s32[1,96]{1,0:T(1,128)S(1)}, s32[1,96]{1,0:T(1,128)S(1)}, u32[]{:S(2)}, u32[]{:S(2)}) collective-permute-start(s32[1,96]{1,0:T(1,128)S(1)} %collective-permute-done.11.target_one), channel_id=1, source_target_pairs={{0,1},{1,0},{2,3},{3,2},{4,5},{5,4},{6,7},{7,6},{8,9},{9,8},{10,11... | collective-permute-start | bytes 1160 | tf_op jit(solution)/shard_map/ppermute | solution.py:376
  85.4 11.5 %copy-start.1 = (s32[192,1]{0,1:T(1,128)S(1)}, s32[192,1]{0,1:T(1,128)}, u32[]{:S(2)}) copy-start(s32[192,1]{0,1:T(1,128)} %param.10) | copy-start | bytes 2308
  85.4 11.5 %copy-start.3 = (f32[8]{0:T(128)S(1)}, f32[8]{0:T(128)}, u32[]{:S(2)}) copy-start(f32[8]{0:T(128)} %param.11) | copy-start | bytes 100
  85.4 11.5 %copy-start.4 = (f32[8]{0:T(128)S(1)}, f32[8]{0:T(128)}, u32[]{:S(2)}) copy-start(f32[8]{0:T(128)} %param.12) | copy-start | bytes 100
  85.4 27.3 %copy-start.5 = (s32[16]{0:T(128)S(1)}, s32[16]{0:T(128)}, u32[]{:S(2)}) copy-start(s32[16]{0:T(128)} %param.13) | copy-start | bytes 196
  85.5 11.5 %collective-permute-start.14 = (f32[8,256]{1,0:T(8,128)S(1)}, f32[8,256]{1,0:T(8,128)S(1)}, u32[]{:S(2)}, u32[]{:S(2)}) collective-permute-start(f32[8,256]{1,0:T(8,128)S(1)} %get-tuple-element.47), channel_id=1, source_target_pairs={{0,1},{1,0},{2,3},{3,2},{4,5},{5,4},{6,7},{7,6},{8,9},{9,8},{10,11... | collective-permute-start | bytes 24584 | tf_op jit(solution)/shard_map/ppermute | solution.py:376
